TPU v7x, 512 devices: a whole 4x8x8 slice. The times are simulated.
512 devices in a mesh: dom: 64 (over z, x, core), rep: 8 (over y).
Axes of the slice: x: 4, y: 8, z: 8, core: 2. Of those that a mesh axis runs over, the one named last changes fastest.
Arguments:
- features: bfloat16 [65536, 256], P('dom'), may hold values from -6 to 6
- weight: bfloat16 [256, 256], replicated, may hold values from -0.375 to 0.375
- adjacency: bfloat16 [64, 8, 16, 128, 128], P('dom', 'rep'), may hold values from -0.21875 to 0.21875
- tile_row: int32 [64, 8, 16], P('dom', 'rep'), may hold values from 0 to 7
- tile_column: int32 [64, 8, 16], P('dom', 'rep'), may hold values from 0 to 15
- tile_counts: int32 [64, 8], P('dom', 'rep'), may hold values from 2 to 16, as said below
- send_rows: int32 [64, 8, 64, 16], P('dom', 'rep'), may hold values from 0 to 1023
- send_counts: int32 [64, 8, 64], P('dom', 'rep'), may hold values from 0 to 16, as said below
- cotangent: bfloat16 [65536, 256], P(('dom', 'rep')), may hold values from -24 to 24
Outputs:
- output: bfloat16 [65536, 256], P(('dom', 'rep'))
- feature_grad: bfloat16 [65536, 256], P(('dom', 'rep'))
- weight_grad: float32 [256, 256], P('rep')
Inputs may be any that keep to these rules, and one draw needn't show every extreme that they name: Slots t >= tile_counts of a device are padding; one device has all 16 slots live. `send_counts`: A partition sends nothing to itself; every partition at every replica index fills all 16 slots for at least one other partition.
All inputs are finite; a program needn't handle non-finite values.
Results may differ from a plain program's by a relative error of at most 0.0061.
Values may be sent and summed in bfloat16 or wider, within the bound.
A program may use at most 64 MiB of HBM per device.

v0:
```python
import jax
import jax.numpy as jnp
from jax import lax
from jax.sharding import PartitionSpec as P

GELU_SCALE = 0.7978845608028654
GELU_CUBIC = 0.044715


def gelu_pair(pre_act):
    inner_arg = GELU_SCALE * (pre_act + GELU_CUBIC * pre_act * pre_act * pre_act)
    tanh_part = jnp.tanh(inner_arg)
    activated = 0.5 * pre_act * (1.0 + tanh_part)
    derivative = 0.5 * (1.0 + tanh_part) + 0.5 * pre_act * (
        1.0 - tanh_part * tanh_part
    ) * GELU_SCALE * (1.0 + 3.0 * GELU_CUBIC * pre_act * pre_act)
    return (activated, derivative)


def local(
    features,
    weight,
    adjacency,
    tile_row,
    tile_column,
    tile_counts,
    send_rows,
    send_counts,
    cotangent,
):
    rows_total, hidden = features.shape
    partitions = lax.axis_size("dom")
    groups = lax.axis_size("rep")
    rep_index = lax.axis_index("rep")
    tile_vals = adjacency[0, 0]
    tile_edge = tile_vals.shape[-1]
    row_index = tile_row[0, 0]
    column_index = tile_column[0, 0]
    live_tiles = tile_counts[0, 0]
    row_lists = send_rows[0, 0]
    list_counts = send_counts[0, 0]
    capacity = row_lists.shape[1]
    local_rows = rows_total // groups
    slot_live = jnp.arange(capacity)[None, :] < list_counts[:, None]
    outgoing = jnp.where(slot_live[..., None], features[row_lists], jnp.zeros((), features.dtype))
    incoming = lax.all_to_all(outgoing, "dom", split_axis=0, concat_axis=0, tiled=True)
    combined = jnp.concatenate([features, incoming.reshape(partitions * capacity, hidden)], 0)
    col_tiles = combined.shape[0] // tile_edge
    space_tiles = combined.reshape(col_tiles, tile_edge, hidden)
    row_tiles = rows_total // tile_edge
    block_size = 16
    blocks = (live_tiles + block_size - 1) // block_size

    def block_parts(block_number):
        start = block_number * block_size
        is_live = start + jnp.arange(block_size) < live_tiles
        return (tile_vals, row_index, column_index, is_live)

    def forward_block(block_number, running):
        block_vals, block_rows, block_columns, is_live = block_parts(block_number)
        picked = space_tiles[block_columns]
        products = jnp.einsum(
            "tij,tjf->tif", block_vals, picked, preferred_element_type=jnp.float32
        )
        onehot = (
            (block_rows[None, :] == jnp.arange(row_tiles)[:, None]) & is_live[None, :]
        ).astype(jnp.float32)
        return running + jnp.dot(
            onehot,
            products.reshape(block_size, tile_edge * hidden),
            precision=lax.Precision.HIGHEST,
        )

    partial_value = lax.fori_loop(
        0, blocks, forward_block, jnp.zeros((row_tiles, tile_edge * hidden), jnp.float32)
    )
    partial_value = partial_value.reshape(rows_total, hidden)
    aggregate_all = lax.psum(partial_value, "rep").astype(jnp.bfloat16)
    pre_all = jnp.einsum("ni,oi->no", aggregate_all, weight, preferred_element_type=jnp.float32)
    activated, derivative = gelu_pair(pre_all)
    full_cot = lax.all_gather(cotangent, "rep", axis=0, tiled=True)
    output = lax.dynamic_slice_in_dim(activated, rep_index * local_rows, local_rows, 0).astype(
        jnp.bfloat16
    )
    grad_all = (full_cot.astype(jnp.float32) * derivative).astype(jnp.bfloat16)
    row_grad = jnp.dot(grad_all, weight, preferred_element_type=jnp.float32).astype(jnp.bfloat16)
    aggregate_own = lax.dynamic_slice_in_dim(aggregate_all, rep_index * local_rows, local_rows, 0)
    grad_own = lax.dynamic_slice_in_dim(grad_all, rep_index * local_rows, local_rows, 0)
    weight_part = jnp.einsum(
        "no,ni->oi", grad_own, aggregate_own, preferred_element_type=jnp.float32
    )
    grad_tiles = row_grad.reshape(row_tiles, tile_edge, hidden)

    def backward_block(block_number, running):
        block_vals, block_rows, block_columns, is_live = block_parts(block_number)
        picked = grad_tiles[block_rows]
        products = jnp.einsum(
            "tij,tif->tjf", block_vals, picked, preferred_element_type=jnp.float32
        )
        onehot = (
            (block_columns[None, :] == jnp.arange(col_tiles)[:, None]) & is_live[None, :]
        ).astype(jnp.float32)
        return running + jnp.dot(
            onehot,
            products.reshape(block_size, tile_edge * hidden),
            precision=lax.Precision.HIGHEST,
        )

    space_grad = lax.fori_loop(
        0, blocks, backward_block, jnp.zeros((col_tiles, tile_edge * hidden), jnp.float32)
    )
    space_grad = space_grad.reshape(col_tiles * tile_edge, hidden)
    halo_grads = space_grad[rows_total:].reshape(partitions, capacity, hidden)
    returned = lax.all_to_all(halo_grads, "dom", split_axis=0, concat_axis=0, tiled=True)
    returned = jnp.where(slot_live[..., None], returned, jnp.zeros((), returned.dtype))
    feature_part = (
        space_grad[:rows_total]
        .at[row_lists.reshape(-1)]
        .add(returned.reshape(partitions * capacity, hidden))
    )
    feature_share = lax.psum_scatter(feature_part, "rep", scatter_dimension=0, tiled=True)
    weight_total = lax.psum(weight_part, ("dom", "rep"))
    weight_rows = lax.dynamic_slice_in_dim(
        weight_total, rep_index * (hidden // groups), hidden // groups, 0
    )
    weight_grad = weight_rows * float(rows_total * partitions) ** (-0.5)
    return (output, feature_share.astype(jnp.bfloat16), weight_grad)


def solution(mesh):
    in_specs = (
        P("dom", None),
        P(),
        P("dom", "rep", None, None, None),
        P("dom", "rep", None),
        P("dom", "rep", None),
        P("dom", "rep"),
        P("dom", "rep", None, None),
        P("dom", "rep", None),
        P(("dom", "rep"), None),
    )
    out_specs = (P(("dom", "rep"), None), P(("dom", "rep"), None), P("rep", None))
    return jax.shard_map(local, mesh=mesh, in_specs=in_specs, out_specs=out_specs, check_vma=False)
```

profile of v0, /device:TPU:1, one launch (start us, length us, event | category | flops | bytes accessed | tf_op | source)
XLA Modules:
  0.0 434.7 jit_solution(12657082004993802783)
XLA Ops:
  8.0 0.8 iota_compare_fusion.2
  8.8 0.7 compare_select_fusion.2
  9.7 4.6 %gather_fusion.1 = bf16[1024,256]{1,0:T(8,128)(2,1)S(1)} fusion(bf16[1024,256]{1,0:T(8,128)(2,1)} %param.13, s32[1024]{0:T(1024)S(1)} %broadcast_clamp_fusion), kind=kCustom, calls=%fused_computation.1 | custom fusion | bytes 1052672 | tf_op jit(solution)/shard_map/gather | solution.py:45
  14.3 1.0 broadcast_select_fusion.1
  15.3 14.8 %all-to-all-start = ((bf16[64,16,256]{2,1,0:T(8,128)(2,1)}), bf16[64,16,256]{2,1,0:T(8,128)(2,1)S(1)}, u32[]{:S(2)}, u32[]{:S(2)}) async-start(bf16[64,16,256]{2,1,0:T(8,128)(2,1)} %broadcast_select_fusion.1), calls=%async_computation | async-start | bytes 1048576 | tf_op jit(solution)/shard_map/all_to_all | solution.py:46
  30.8 22.1 %all_gather.3 = bf16[1024,256]{1,0:T(8,128)(2,1)S(1)} all-gather(bf16[128,256]{1,0:T(8,128)(2,1)S(1)} %copy-done.6), channel_id=1, replica_groups=mesh['dom'=64,'rep'=8] {'rep'}, dimensions={0}, use_global_device_ids=true | all-gather | bytes 589824 | tf_op jit(solution)/shard_map/all_gather | solution.py:81
  53.0 0.6 gather_fusion.2
  54.0 3.5 while.22
  54.0 0.7 add_compare_fusion.4
  55.1 1.2 copy.23
  56.3 1.2 convolution_add_fusion.4
  57.7 48.5 %all-reduce.4 = bf16[1024,256]{1,0:T(8,128)(2,1)S(1)} all-reduce(f32[1024,256]{1,0:T(8,128)S(1)} %reshape.179), channel_id=1, replica_groups=mesh['dom'=64,'rep'=8] {'rep'}, use_global_device_ids=true, to_apply=%region_2.3 | all-reduce | flops 262144 | bytes 1572864 | tf_op jit(solution)/shard_map/psum | solution.py:78
  106.2 2.2 fusion.15
  108.4 0.8 copy-done.5
  109.5 1.5 broadcast_in_dim.42
  111.0 9.4 %while.23 = (s32[]{:T(128)}, f32[16,32768]{1,0:T(8,128)}, s32[]{:T(128)}, s32[1,1,16]{2,1,0:T(1,128)S(1)}, s32[]{:T(128)}, /*index=5*/s32[16]{0:T(128)S(1)}, bf1...) while((s32[]{:T(128)}, f32[16,32768]{1,0:T(8,128)}, s32[]{:T(128)}, ...), condition=%wide.region_4.5_spmd, body=%wide.region_3.4_spmd.sunk | while | flops 235406928 | bytes 16257497 | solution.py:109
  111.0 0.7 add_compare_fusion.5
  111.7 0.6 gather_fusion
  112.3 1.8 convolution_bitcast_fusion.2
  114.1 2.2 copy.24
  116.3 4.1 convolution_add_fusion.5
  120.4 1.7 fusion.23
  122.0 1.1 reshape.181
  123.2 26.5 %all-to-all-start.1 = ((f32[64,16,256]{2,1,0:T(8,128)}), f32[64,16,256]{2,1,0:T(8,128)S(1)}, u32[]{:S(2)}, u32[]{:S(2)}) async-start(f32[64,16,256]{2,1,0:T(8,128)} %reshape.181), calls=%async_computation.1 | async-start | bytes 2097152 | tf_op jit(solution)/shard_map/all_to_all | solution.py:114
  149.9 1.8 fusion.18
  152.0 25.7 %all-to-all-done.1 = f32[64,16,256]{2,1,0:T(8,128)S(1)} async-done(((f32[64,16,256]{2,1,0:T(8,128)}), f32[64,16,256]{2,1,0:T(8,128)S(1)}, u32[]{:S(2)}, u32[]{:S(2)}) %all-to-all-start.1) | async-done | bytes 1048608 | tf_op jit(solution)/shard_map/all_to_all | solution.py:114
  177.9 6.6 %scatter_fusion = f32[1024,256]{1,0:T(8,128)S(1)} fusion(f32[1024,256]{1,0:T(8,128)S(1)} %slice.11, s32[1024]{0:T(1024)S(1)} %bitcast.84, f32[1024,256]{1,0:T(8,128)S(1)} %bitcast.80), kind=kCustom, calls=%fused_computation.3 | custom fusion | flops 262144 | bytes 3149824 | tf_op jit(solution)/shard_map/scatter-add | solution.py:119
  184.6 1.0 copy-done.1
  185.6 1.6 fusion.17
  187.2 237.1 %all-reduce.3.cloned.1.call-done = f32[256,256]{1,0:T(8,128)} async-done(((f32[256,256]{1,0:T(8,128)}), f32[256,256]{1,0:T(8,128)}) %all-reduce.3.cloned.1.call-update) | async-done | bytes 262160 | tf_op jit(solution)/shard_map/psum | solution.py:122
  424.3 1.4 dynamic-slice_multiply_fusion.1
  425.7 1.5 convert_element_type.25
  (41 shorter events, 2.2 us)
Async XLA Ops:
  8.0 98.2 %copy-start = (bf16[256,256]{1,0:T(8,128)(2,1)S(1)}, bf16[256,256]{1,0:T(8,128)(2,1)}, u32[]{:S(2)}) copy-start(bf16[256,256]{1,0:T(8,128)(2,1)} %param.14) | copy-start | bytes 393220
  14.2 16.6 %copy-start.9 = (s32[1,1,16]{2,1,0:T(1,128)S(1)}, s32[1,1,16]{2,1,0:T(1,128)}, u32[]{:S(2)}) copy-start(s32[1,1,16]{2,1,0:T(1,128)} %param.17) | copy-start | bytes 196
  14.3 16.6 %copy-start.6 = (bf16[128,256]{1,0:T(8,128)(2,1)S(1)}, bf16[128,256]{1,0:T(8,128)(2,1)}, u32[]{:S(2)}) copy-start(bf16[128,256]{1,0:T(8,128)(2,1)} %param.21) | copy-start | bytes 196612
  14.3 38.6 %copy-start.3 = (bf16[1024,256]{1,0:T(8,128)(2,1)S(1)}, bf16[1024,256]{1,0:T(8,128)(2,1)}, u32[]{:S(2)}) copy-start(bf16[1024,256]{1,0:T(8,128)(2,1)} %param.13) | copy-start | bytes 1572868
  15.3 37.6 %all-to-all-start = ((bf16[64,16,256]{2,1,0:T(8,128)(2,1)}), bf16[64,16,256]{2,1,0:T(8,128)(2,1)S(1)}, u32[]{:S(2)}, u32[]{:S(2)}) async-start(bf16[64,16,256]{2,1,0:T(8,128)(2,1)} %broadcast_select_fusion.1), calls=%async_computation | async-start | bytes 1048576 | tf_op jit(solution)/shard_map/all_to_all | solution.py:46
  53.0 1.0 copy-start.2
  53.0 1.0 copy-start.8
  106.2 2.2 copy-start.4
  108.4 0.8 copy-start.5
  122.0 27.7 %copy-start.7 = (s32[1,1,64,16]{2,3,1,0:T(8,128)S(1)}, s32[1,1,64,16]{2,3,1,0:T(8,128)}, u32[]{:S(2)}) copy-start(s32[1,1,64,16]{2,3,1,0:T(8,128)} %param.19) | copy-start | bytes 12292
  123.2 54.5 %all-to-all-start.1 = ((f32[64,16,256]{2,1,0:T(8,128)}), f32[64,16,256]{2,1,0:T(8,128)S(1)}, u32[]{:S(2)}, u32[]{:S(2)}) async-start(f32[64,16,256]{2,1,0:T(8,128)} %reshape.181), calls=%async_computation.1 | async-start | bytes 2097152 | tf_op jit(solution)/shard_map/all_to_all | solution.py:114
  149.7 274.7 %all-reduce.3.cloned.1.call-start = ((), (), s32[]{:S(2)}) async-start(), calls=%async_computation.4 | async-start | bytes 524288 | tf_op jit(solution)/shard_map/psum | solution.py:122
  151.8 273.9 %reduce-scatter.2.cloned.1.call-start = ((), (), s32[]{:S(2)}) async-start(), calls=%async_computation.3 | async-start | bytes 1179648 | tf_op jit(solution)/shard_map/reduce_scatter | solution.py:121
  184.6 1.0 copy-start.1
Sparse Core Ops, SparseCore 0:
  155.5 268.7 all-reduce.2
Sparse Core Ops, SparseCore 1:
  185.6 31.5 reduce-scatter.1
where the time goes:
time: 435 us
  waiting for transfers between devices  263 us (60%)
  blocking collectives  70.6 us (16%)
  starting transfers between devices  41.4 us (10%)
  between operations  16.4 us (4%)
  local copies, waits for them, and re-layouts  16.3 us (4%)
  other arithmetic  15.3 us (4%)
  matrix products  11.7 us (3%)
    psum x1, waiting for transfers between devices, local(): weight_total = lax.psum(weight_part, ('dom', 'rep'))  237 us
    psum x1, blocking collectives, local(): aggregate_all = lax.psum(partial_value, 'rep').astype(jnp.bfloat16)  48.5 us
    all_to_all x1, starting transfers between devices, local(): lax.all_to_all(halo_grads, 'dom', split_axis=0, concat_axis=0, tiled=True)  26.5 us
    all_to_all x1, waiting for transfers between devices, local(): lax.all_to_all(halo_grads, 'dom', split_axis=0, concat_axis=0, tiled=True)  25.7 us
    all_gather x1, blocking collectives, local(): full_cot = lax.all_gather(cotangent, 'rep', axis=0, tiled=True)  22.1 us
    all_to_all x1, starting transfers between devices, local(): lax.all_to_all(outgoing, 'dom', split_axis=0, concat_axis=0, tiled=True)  14.8 us
  transfers between devices with their start and end apart: 4, of which 2 were waited for; matrix products, arithmetic and copies ran while one was open for 3% of the time, Pallas kernels for 0%

commit v1 on v0

v1 whole, which is shorter than its diff:
```python
import functools

import jax
import jax.numpy as jnp
from jax import lax
from jax.experimental import pallas as pl
from jax.experimental.pallas import tpu as pltpu
from jax.sharding import PartitionSpec as P

GELU_SCALE = 0.7978845608028654
GELU_CUBIC = 0.044715
MESH = pl.DeviceIdType.MESH
TILE = 128
CAP = 16
F32 = jnp.float32
BF16 = jnp.bfloat16


def gelu_pair(pre_act):
    inner_arg = GELU_SCALE * (pre_act + GELU_CUBIC * pre_act * pre_act * pre_act)
    tanh_part = jnp.tanh(inner_arg)
    activated = 0.5 * pre_act * (1.0 + tanh_part)
    derivative = 0.5 * (1.0 + tanh_part) + 0.5 * pre_act * (
        1.0 - tanh_part * tanh_part
    ) * GELU_SCALE * (1.0 + 3.0 * GELU_CUBIC * pre_act * pre_act)
    return (activated, derivative)


def loop(start, stop, body):
    def step(k, carry):
        body(k)
        return carry

    lax.fori_loop(start, stop, step, 0)


def kernel(
    doms,
    reps,
    scale,
    features,
    weight,
    adjacency,
    slots,
    tile_row,
    tile_column,
    tile_count,
    cotangent,
    output,
    feature_grad,
    weight_grad,
    space,
    outgoing,
    scatter,
    a_cat,
    at_cat,
    row_lanes,
    column_lanes,
    picked,
    agg_send,
    agg_recv,
    row_grads,
    back_send,
    back_recv,
    feature_part,
    feat_send,
    feat_recv,
    w_send,
    w_recv,
    w_sum,
    w_rep,
    w_done,
    send_sems,
    recv_sems,
):
    d = lax.axis_index("dom")
    r = lax.axis_index("rep")
    rows, hidden = features.shape
    tiles = adjacency.shape[0]
    row_tiles = rows // TILE
    blocks = doms * CAP // TILE
    per = TILE // CAP
    first_halo = rows // CAP
    HALO, AGG, GRAD, BACK, FEAT, W_DOM, W_REP, W_END = range(8)

    barrier = pltpu.get_barrier_semaphore()

    def greet_dom(k):
        pl.semaphore_signal(
            barrier, inc=1, device_id={"dom": lax.rem(d + k, doms)}, device_id_type=MESH
        )

    def greet_rep(k):
        pl.semaphore_signal(
            barrier, inc=1, device_id={"rep": lax.rem(r + k, reps)}, device_id_type=MESH
        )

    loop(1, doms, greet_dom)
    loop(1, reps, greet_rep)

    def push(src, dst, phase, target):
        pltpu.make_async_remote_copy(
            src_ref=src,
            dst_ref=dst,
            send_sem=send_sems.at[phase],
            recv_sem=recv_sems.at[phase],
            device_id=target,
            device_id_type=MESH,
        ).start()

    def await_bytes(ref, sems, phase):
        pltpu.make_async_copy(ref, ref, sems.at[phase]).wait()

    def send_block(block, src, dst, phase):
        def send(j):
            q = block * per + j

            @pl.when(q != d)
            def _():
                push(src.at[q], dst, phase, {"dom": q})

        loop(0, per, send)

    lane = lax.broadcasted_iota(jnp.int32, (TILE, TILE), 1)

    def gather(b):
        block = lax.rem(d // per + b, blocks)
        listed = jnp.broadcast_to(slots[pl.ds(block, 1), :], (TILE, TILE)).T
        onehot = jnp.concatenate(
            [jnp.where(listed == lane + i * TILE, 1.0, 0.0).astype(BF16) for i in range(row_tiles)],
            axis=1,
        )
        picked_rows = jnp.dot(onehot, features[...], preferred_element_type=F32).astype(BF16)
        outgoing[pl.ds(block * per, per)] = picked_rows.reshape(per, CAP, hidden)

    gather(0)
    pl.semaphore_wait(barrier, doms + reps - 2)
    send_block(d // per, outgoing, space.at[first_halo + d], HALO)

    def gather_and_send(b):
        gather(b)
        send_block(lax.rem(d // per + b, blocks), outgoing, space.at[first_halo + d], HALO)

    loop(1, blocks, gather_and_send)

    space[pl.ds(0, first_halo)] = features[...].reshape(first_halo, CAP, hidden)
    space[first_halo + d] = jnp.zeros((CAP, hidden), BF16)
    back_recv[d] = jnp.zeros((CAP, hidden), BF16)
    for t in range(tiles):
        lanes = slice(t * TILE, (t + 1) * TILE)
        live = t < tile_count[0]
        row_lanes[:, lanes] = jnp.full((CAP, TILE), jnp.where(live, tile_row[t], -1), jnp.int32)
        column_lanes[:, lanes] = jnp.full(
            (CAP, TILE), jnp.where(live, tile_column[t], -1), jnp.int32
        )
        a_cat[:, :, lanes] = adjacency[t].reshape(per, CAP, TILE)
        at_cat[:, :, lanes] = adjacency[t].T.reshape(per, CAP, TILE)
    row = lax.broadcasted_iota(jnp.int32, (TILE, TILE), 0)

    def make_scatter(i):
        for block in range(blocks):
            listed = jnp.broadcast_to(slots[block : block + 1, :], (TILE, TILE))
            scatter[i, :, block * TILE : (block + 1) * TILE] = jnp.where(
                listed == row + i * TILE, 1.0, 0.0
            ).astype(BF16)

    loop(0, row_tiles, make_scatter)

    def tile_sum(values, lanes, index):
        mask = jnp.where(lanes[...] == index, 1.0, 0.0).astype(BF16)
        masked = (values[...] * mask[None]).reshape(TILE, tiles * TILE)
        return jnp.dot(masked, picked[...], preferred_element_type=F32)

    await_bytes(space.at[pl.ds(first_halo, doms - 1)], recv_sems, HALO)
    for t in range(tiles):
        picked[t * TILE : (t + 1) * TILE, :] = space[pl.ds(tile_column[t] * per, per)].reshape(
            TILE, hidden
        )

    def forward(k):
        i = lax.rem(r + k, reps)
        agg_send[i] = tile_sum(a_cat, row_lanes, i).astype(BF16)
        push(agg_send.at[i], agg_recv.at[r], AGG, {"rep": i})

    loop(1, reps, forward)
    total = tile_sum(a_cat, row_lanes, r)
    await_bytes(agg_recv.at[pl.ds(0, reps - 1)], recv_sems, AGG)
    for k in range(1, reps):
        total = total + agg_recv[lax.rem(r + k, reps)].astype(F32)
    aggregate = total.astype(BF16)

    pre_act = lax.dot_general(
        aggregate, weight[...], (((1,), (1,)), ((), ())), preferred_element_type=F32
    )
    activated, derivative = gelu_pair(pre_act)
    pre_grad = (cotangent[...].astype(F32) * derivative).astype(BF16)
    row_grads[r] = jnp.dot(pre_grad, weight[...], preferred_element_type=F32).astype(BF16)

    def share_rows(k):
        push(row_grads.at[r], row_grads.at[r], GRAD, {"rep": lax.rem(r + k, reps)})

    loop(1, reps, share_rows)
    output[...] = activated.astype(BF16)

    w_part = lax.dot_general(
        pre_grad, aggregate, (((0,), (0,)), ((), ())), preferred_element_type=F32
    )
    chunk = w_send.shape[1]
    half = doms // 2
    for h in range(2):
        w_send[h * half : (h + 1) * half] = w_part[:, h * TILE : (h + 1) * TILE].reshape(
            half, chunk, TILE
        )

    def share_weight(k):
        q = lax.rem(d + k, doms)
        push(w_send.at[q], w_recv.at[d], W_DOM, {"dom": q})

    loop(1, doms, share_weight)
    w_recv[d] = w_send[d]

    await_bytes(row_grads.at[pl.ds(0, reps - 1)], recv_sems, GRAD)
    for t in range(tiles):
        picked[t * TILE : (t + 1) * TILE, :] = row_grads[tile_row[t]]

    def backward_halo(b):
        block = lax.rem(d // per + b, blocks)
        grads = tile_sum(at_cat, column_lanes, block + row_tiles).astype(BF16)
        back_send[pl.ds(block * per, per)] = grads.reshape(per, CAP, hidden)
        send_block(block, back_send, back_recv.at[d], BACK)

    loop(0, blocks, backward_halo)

    spread = half // reps
    holder = lax.rem(d, half) // spread
    place = (d // half) * spread + lax.rem(d, spread)
    await_bytes(w_recv.at[pl.ds(0, doms - 1)], recv_sems, W_DOM)
    w_sum[...] = jnp.sum(w_recv[...], axis=0)

    @pl.when(r != holder)
    def _():
        push(w_sum, w_rep.at[r], W_REP, {"rep": holder})

    def backward_local(i):
        feature_part[i] = tile_sum(at_cat, column_lanes, i)

    loop(0, row_tiles, backward_local)

    @pl.when(r == holder)
    def _():
        await_bytes(w_rep.at[pl.ds(0, reps - 1)], recv_sems, W_REP)
        whole = w_sum[...]
        for k in range(1, reps):
            whole = whole + w_rep[lax.rem(r + k, reps)]
        w_done[place] = whole * scale

        def share_done(k):
            push(w_done.at[place], w_done.at[place], W_END, {"dom": lax.rem(d + k, doms)})

        loop(1, doms, share_done)

    await_bytes(back_recv.at[pl.ds(0, doms - 1)], recv_sems, BACK)

    def feature_rows(i):
        returned = back_recv[...].reshape(doms * CAP, hidden)
        return feature_part[i] + jnp.dot(scatter[i], returned, preferred_element_type=F32)

    def feature(k):
        i = lax.rem(r + k, reps)
        feat_send[i] = feature_rows(i).astype(BF16)
        push(feat_send.at[i], feat_recv.at[r], FEAT, {"rep": i})

    loop(1, reps, feature)
    own = feature_rows(r)

    @pl.when(r == holder)
    def _():
        await_bytes(w_done.at[pl.ds(0, 2 * spread - 1)], recv_sems, W_END)

    @pl.when(r != holder)
    def _():
        await_bytes(w_done, recv_sems, W_END)

    for h in range(2):
        weight_grad[:, h * TILE : (h + 1) * TILE] = w_done[h * spread : (h + 1) * spread].reshape(
            spread * chunk, TILE
        )

    await_bytes(feat_recv.at[pl.ds(0, reps - 1)], recv_sems, FEAT)
    for k in range(1, reps):
        own = own + feat_recv[lax.rem(r + k, reps)].astype(F32)
    feature_grad[...] = own.astype(BF16)

    await_bytes(outgoing.at[pl.ds(0, doms - 1)], send_sems, HALO)
    await_bytes(agg_send.at[pl.ds(0, reps - 1)], send_sems, AGG)
    await_bytes(row_grads.at[pl.ds(0, reps - 1)], send_sems, GRAD)
    await_bytes(back_send.at[pl.ds(0, doms - 1)], send_sems, BACK)
    await_bytes(feat_send.at[pl.ds(0, reps - 1)], send_sems, FEAT)
    await_bytes(w_send.at[pl.ds(0, doms - 1)], send_sems, W_DOM)

    @pl.when(r != holder)
    def _():
        await_bytes(w_sum, send_sems, W_REP)

    @pl.when(r == holder)
    def _():
        await_bytes(w_send.at[pl.ds(0, doms - 1)], send_sems, W_END)


def solution(mesh):
    doms, reps = mesh.shape["dom"], mesh.shape["rep"]

    def local(
        features,
        weight,
        adjacency,
        tile_row,
        tile_column,
        tile_counts,
        send_rows,
        send_counts,
        cotangent,
    ):
        rows, hidden = features.shape
        tiles = adjacency.shape[2]
        row_tiles = rows // TILE
        blocks = doms * CAP // TILE
        chunk = 2 * hidden // doms
        slot_live = jnp.arange(CAP)[None, :] < send_counts[0, 0][:, None]
        slots = jnp.where(slot_live, send_rows[0, 0], -1).reshape(blocks, TILE)
        vmem = pl.BlockSpec(memory_space=pltpu.VMEM)
        smem = pl.BlockSpec(memory_space=pltpu.SMEM)
        return pl.pallas_call(
            functools.partial(kernel, doms, reps, float(rows * doms) ** (-0.5)),
            out_shape=(
                jax.ShapeDtypeStruct((rows // reps, hidden), BF16),
                jax.ShapeDtypeStruct((rows // reps, hidden), BF16),
                jax.ShapeDtypeStruct((hidden // reps, hidden), F32),
            ),
            in_specs=[vmem] * 4 + [smem] * 3 + [vmem],
            out_specs=(vmem, vmem, vmem),
            scratch_shapes=[
                pltpu.VMEM((rows // CAP + doms, CAP, hidden), BF16),
                pltpu.VMEM((doms, CAP, hidden), BF16),
                pltpu.VMEM((row_tiles, TILE, doms * CAP), BF16),
                pltpu.VMEM((TILE // CAP, CAP, tiles * TILE), BF16),
                pltpu.VMEM((TILE // CAP, CAP, tiles * TILE), BF16),
                pltpu.VMEM((CAP, tiles * TILE), jnp.int32),
                pltpu.VMEM((CAP, tiles * TILE), jnp.int32),
                pltpu.VMEM((tiles * TILE, hidden), BF16),
                pltpu.VMEM((reps, TILE, hidden), BF16),
                pltpu.VMEM((reps, TILE, hidden), BF16),
                pltpu.VMEM((reps, TILE, hidden), BF16),
                pltpu.VMEM((doms, CAP, hidden), BF16),
                pltpu.VMEM((doms, CAP, hidden), BF16),
                pltpu.VMEM((row_tiles, TILE, hidden), F32),
                pltpu.VMEM((reps, TILE, hidden), BF16),
                pltpu.VMEM((reps, TILE, hidden), BF16),
                pltpu.VMEM((doms, chunk, TILE), F32),
                pltpu.VMEM((doms, chunk, TILE), F32),
                pltpu.VMEM((chunk, TILE), F32),
                pltpu.VMEM((reps, chunk, TILE), F32),
                pltpu.VMEM((doms // reps, chunk, TILE), F32),
                pltpu.SemaphoreType.DMA((8,)),
                pltpu.SemaphoreType.DMA((8,)),
            ],
            compiler_params=pltpu.CompilerParams(
                collective_id=0, has_side_effects=True, vmem_limit_bytes=40 * 2**20
            ),
        )(
            features,
            weight,
            adjacency[0, 0],
            slots,
            tile_row[0, 0],
            tile_column[0, 0],
            tile_counts[0],
            cotangent,
        )

    in_specs = (
        P("dom", None),
        P(),
        P("dom", "rep", None, None, None),
        P("dom", "rep", None),
        P("dom", "rep", None),
        P("dom", "rep"),
        P("dom", "rep", None, None),
        P("dom", "rep", None),
        P(("dom", "rep"), None),
    )
    out_specs = (P(("dom", "rep"), None), P(("dom", "rep"), None), P("rep", None))
    return jax.shard_map(local, mesh=mesh, in_specs=in_specs, out_specs=out_specs, check_vma=False)
```

time: 435 us -> 103 us (0.24)
  waiting for transfers between devices: 263 us -> 0 us
  Pallas kernels: 0 us -> 91.8 us
  blocking collectives: 70.6 us -> 0 us
  starting transfers between devices: 41.4 us -> 0 us
  between operations: 16.4 us -> 1.36 us
  other arithmetic: 15.3 us -> 1.32 us
  matrix products: 11.7 us -> 0 us
  local copies, waits for them, and re-layouts: 16.3 us -> 7.14 us
    psum x1 -> x0, waiting for transfers between devices: 237 us -> none  [local(): weight_total = lax.psum(weight_part, ('dom', 'rep'))]
    pallas_call x0 -> x1, Pallas kernels: none -> 91.8 us  [local(): pl.pallas_call(functools.partial(kernel, doms, reps, float(rows * doms) *...]
    psum x1 -> x0, blocking collectives: 48.5 us -> none  [local(): aggregate_all = lax.psum(partial_value, 'rep').astype(jnp.bfloat16)]
    all_to_all x2 -> x0, starting transfers between devices: 41.3 us -> none  [the longest x1 26.5 us: local(): lax.all_to_all(halo_grads, 'dom', split_axis=0, concat_axis=0, tiled=True)]
    all_to_all x2 -> x0, waiting for transfers between devices: 25.7 us -> none  [the longest x1 25.7 us: local(): lax.all_to_all(halo_grads, 'dom', split_axis=0, concat_axis=0, tiled=True)]
    all_gather x1 -> x0, blocking collectives: 22.1 us -> none  [local(): full_cot = lax.all_gather(cotangent, 'rep', axis=0, tiled=True)]
    dot_general x7 -> x0, matrix products: 11.7 us -> none  [the longest x1 4.07 us: backward_block(): jnp.dot(onehot, products.reshape(block_size, tile_edge * hidden), precisi...]
    scatter-add x1 -> x0, other arithmetic: 6.63 us -> none  [local(): feature_part = space_grad[:rows_total].at[row_lists.reshape(-1)].add(retu...]
  transfers between devices with their start and end apart: 4 -> 0, of which waited for: 2 -> 0; matrix products, arithmetic and copies ran while one was open for 3% -> 0% of each run, Pallas kernels for 0% -> 0%
where the time goes in v1:
time: 103 us; the launch traced here: 102 us
  Pallas kernels  91.8 us (89%)
  local copies, waits for them, and re-layouts  7.14 us (7%)
  between operations  1.36 us (1%)
  other arithmetic  1.32 us (1%)
    pallas_call x1, Pallas kernels, local(): pl.pallas_call(functools.partial(kernel, doms, reps, float(rows * doms) *...  91.8 us
    unnamed x17, local copies, waits for them, and re-layouts  6.75 us

profile of v1, /device:TPU:1, one launch (start us, length us, event | category | flops | bytes accessed | tf_op | source)
XLA Modules:
  0.0 101.6 jit_solution(15852706862017337896)
XLA Ops:
  0.6 0.0 copy-start.2
  1.3 0.5 broadcast.7
  1.8 1.3 %reduce.3 = s32[64]{0:T(128)S(1)} reduce(s32[1,1,64]{2,1,0:T(1,128)} %param.16, s32[]{:T(128)} %broadcast.7), dimensions={0,1}, to_apply=%param.16.reduce_sub_computation.3 | reduce | bytes 516 | tf_op args[7]
  3.2 0.1 lt.25
  3.2 0.1 lt.23
  3.3 0.1 lt.26
  3.4 0.1 lt.27
  3.5 0.8 copy.13
  4.3 0.1 squeeze.16
  4.3 0.0 copy-start.4
  4.3 0.0 copy-start.5
  4.4 0.0 copy-done.2
  4.4 0.6 copy-done.4
  5.0 0.0 copy-done.5
  5.0 0.0 copy-start
  5.0 1.0 %copy-done = bf16[1024,256]{1,0:T(8,128)(2,1)S(1)} copy-done((bf16[1024,256]{1,0:T(8,128)(2,1)S(1)}, bf16[1024,256]{1,0:T(8,128)(2,1)}, u32[]{:S(2)}) %copy-start) | copy-done | bytes 524312
  6.1 0.0 copy-start.1
  6.1 1.0 %copy-done.1 = bf16[1,1,16,128,128]{4,3,2,1,0:T(8,128)(2,1)S(1)} copy-done((bf16[1,1,16,128,128]{4,3,2,1,0:T(8,128)(2,1)S(1)}, bf16[1,1,16,128,128]{4,3,2,1,0:T(8,128)(2,1)}, u32[]{:S(2)}) %copy-start.1) | copy-done | bytes 524312
  7.1 0.0 copy-start.3
  7.1 0.8 copy-done.3
  7.9 91.8 %shard_map.112 = (bf16[128,256]{1,0:T(8,128)(2,1)S(1)}, bf16[128,256]{1,0:T(8,128)(2,1)S(1)}, f32[32,256]{1,0:T(8,128)S(1)}) custom-call(bf16[1024,256]{1,0:T(8,128)(2,1)S(1)} %copy-done, bf16[256,256]{1,0:T(8,128)(2,1)S(1)} %copy-done.2, bf16[16,128,128]{2,1,0:T(8,128)(2,1)S(1)} %bitcast.7, s32[8,128]{1,0:T(8,128)S(1)} %compare_select_fusion.slots, ...), custom_call_target="tpu_custom_call" | custom-call | tf_op jit(solution)/shard_map/pallas_call | solution.py:333
  99.8 0.6 copy.18
  100.4 0.6 copy.19
  101.0 0.6 copy.20
  (2 shorter events, 0.0 us)
Async XLA Ops:
  0.6 3.7 %copy-start.2 = (bf16[256,256]{1,0:T(8,128)(2,1)S(1)}, bf16[256,256]{1,0:T(8,128)(2,1)}, u32[]{:S(2)}) copy-start(bf16[256,256]{1,0:T(8,128)(2,1)} %weight.1) | copy-start | bytes 393220
  4.3 0.7 copy-start.4
  4.3 0.7 copy-start.5
  5.0 1.0 %copy-start = (bf16[1024,256]{1,0:T(8,128)(2,1)S(1)}, bf16[1024,256]{1,0:T(8,128)(2,1)}, u32[]{:S(2)}) copy-start(bf16[1024,256]{1,0:T(8,128)(2,1)} %features.1) | copy-start | bytes 1572868
  6.1 1.0 %copy-start.1 = (bf16[1,1,16,128,128]{4,3,2,1,0:T(8,128)(2,1)S(1)}, bf16[1,1,16,128,128]{4,3,2,1,0:T(8,128)(2,1)}, u32[]{:S(2)}) copy-start(bf16[1,1,16,128,128]{4,3,2,1,0:T(8,128)(2,1)} %param.11) | copy-start | bytes 1572868
  7.1 0.8 copy-start.3

commit v2 on v1

v2 whole, which is shorter than its diff:
```python
import functools

import jax
import jax.numpy as jnp
from jax import lax
from jax.experimental import pallas as pl
from jax.experimental.pallas import tpu as pltpu
from jax.sharding import PartitionSpec as P

GELU_SCALE = 0.7978845608028654
GELU_CUBIC = 0.044715
MESH = pl.DeviceIdType.MESH
TILE = 128
CAP = 16
F32 = jnp.float32
BF16 = jnp.bfloat16


def gelu_pair(pre_act):
    inner_arg = GELU_SCALE * (pre_act + GELU_CUBIC * pre_act * pre_act * pre_act)
    tanh_part = jnp.tanh(inner_arg)
    activated = 0.5 * pre_act * (1.0 + tanh_part)
    derivative = 0.5 * (1.0 + tanh_part) + 0.5 * pre_act * (
        1.0 - tanh_part * tanh_part
    ) * GELU_SCALE * (1.0 + 3.0 * GELU_CUBIC * pre_act * pre_act)
    return (activated, derivative)


def loop(start, stop, body):
    def step(k, carry):
        body(k)
        return carry

    lax.fori_loop(start, stop, step, 0)


def kernel(
    doms,
    reps,
    scale,
    features_in,
    weight_in,
    adjacency_in,
    lists_in,
    list_counts_in,
    tile_row_in,
    tile_column_in,
    tile_count_in,
    cotangent_in,
    output,
    feature_grad,
    weight_grad,
    features,
    weight,
    adjacency,
    lists,
    list_counts,
    tile_row,
    tile_column,
    tile_count,
    cotangent,
    listed,
    space_low,
    space_high,
    outgoing,
    scatter,
    a_cat,
    at_cat,
    by_row,
    by_column,
    row_lanes,
    column_lanes,
    picked,
    agg_send,
    agg_recv,
    row_grads_low,
    row_grads_high,
    back_send,
    back_recv,
    feature_part,
    feat_send,
    feat_recv,
    w_send,
    w_recv,
    w_sum,
    w_rep,
    w_done,
    copy_sems,
    send_sems,
    recv_sems,
):
    d = lax.axis_index("dom")
    r = lax.axis_index("rep")
    rows, hidden = features.shape
    tiles = adjacency.shape[0]
    row_tiles = rows // TILE
    blocks = doms * CAP // TILE
    per = TILE // CAP
    first_halo = rows // CAP
    halves = hidden // TILE
    space = (space_low, space_high)
    row_grads = (row_grads_low, row_grads_high)
    HALO, AGG, GRAD, BACK, FEAT = (halves * k for k in range(5))
    W_DOM, W_REP, W_END = (halves * 5 + k for k in range(3))

    barrier = pltpu.get_barrier_semaphore()

    def greet_dom(k):
        pl.semaphore_signal(
            barrier, inc=1, device_id={"dom": lax.rem(d + k, doms)}, device_id_type=MESH
        )

    def greet_rep(k):
        pl.semaphore_signal(
            barrier, inc=1, device_id={"rep": lax.rem(r + k, reps)}, device_id_type=MESH
        )

    loop(1, doms, greet_dom)
    loop(1, reps, greet_rep)

    loads = [
        pltpu.make_async_copy(src, dst, copy_sems.at[k])
        for k, (src, dst) in enumerate(
            (
                (lists_in.at[0, 0], lists),
                (list_counts_in.at[0], list_counts),
                (features_in, features),
                (adjacency_in.at[0, 0], adjacency),
                (tile_row_in, tile_row),
                (tile_column_in, tile_column),
                (tile_count_in, tile_count),
                (weight_in, weight),
                (cotangent_in, cotangent),
            )
        )
    ]
    for load in loads:
        load.start()

    def push(src, dst, phase, target):
        pltpu.make_async_remote_copy(
            src_ref=src,
            dst_ref=dst,
            send_sem=send_sems.at[phase],
            recv_sem=recv_sems.at[phase],
            device_id=target,
            device_id_type=MESH,
        ).start()

    def await_bytes(ref, sems, phase):
        pltpu.make_async_copy(ref, ref, sems.at[phase]).wait()

    def send_block(block, src, dst, phase):
        def send(j):
            q = block * per + j

            @pl.when(q != d)
            def _():
                push(src.at[q], dst, phase, {"dom": q})

        loop(0, per, send)

    def far_block(b):
        step = (2 * lax.rem(b, 2) - 1) * ((b + 1) // 2)
        return lax.rem(d // per + blocks // 2 + step + 2 * blocks, blocks)

    far_reps = sorted(range(1, reps), key=lambda k: -min(k, reps - k))

    lane = lax.broadcasted_iota(jnp.int32, (TILE, TILE), 1)
    row = lax.broadcasted_iota(jnp.int32, (TILE, TILE), 0)
    for load in loads[:3]:
        load.wait()
    slot = lax.broadcasted_iota(jnp.int32, (CAP, doms), 0)
    live_lists = jnp.where(slot < list_counts[...], lists[...], -1)
    for p in range(doms):
        listed[p // per, p % per * CAP : (p % per + 1) * CAP, :] = jnp.broadcast_to(
            live_lists[:, p : p + 1], (CAP, TILE)
        )

    def gather(block):
        rows_of = listed[block]
        onehot = jnp.concatenate(
            [jnp.where(rows_of == lane + i * TILE, 1.0, 0.0).astype(BF16) for i in range(row_tiles)],
            axis=1,
        )
        found = jnp.dot(onehot, features[...], preferred_element_type=F32).astype(BF16)
        for h in range(halves):
            outgoing[h, pl.ds(block * per, per)] = found[:, h * TILE : (h + 1) * TILE].reshape(
                per, CAP, TILE
            )

    def send_halo(block, h):
        send_block(block, outgoing.at[h], space[h].at[first_halo + d], HALO + h)

    gather(far_block(0))
    pl.semaphore_wait(barrier, doms + reps - 2)
    send_halo(far_block(0), 0)

    def gather_and_send(b):
        block = far_block(b)
        gather(block)
        send_halo(block, 0)

    loop(1, blocks, gather_and_send)
    for h in range(1, halves):
        loop(0, blocks, lambda b: send_halo(far_block(b), h))

    for load in loads[3:]:
        load.wait()
    for t in range(tiles):
        lanes = slice(t * TILE, (t + 1) * TILE)
        live = t < tile_count[0, 0]
        row_lanes[:, lanes] = jnp.full(
            (CAP, TILE), jnp.where(live, tile_row[0, 0, t], -1), jnp.int32
        )
        column_lanes[:, lanes] = jnp.full(
            (CAP, TILE), jnp.where(live, tile_column[0, 0, t], -1), jnp.int32
        )
        a_cat[:, :, lanes] = adjacency[t].reshape(per, CAP, TILE)
        at_cat[:, :, lanes] = adjacency[t].T.reshape(per, CAP, TILE)

    def mask_tiles(dst, values, lanes):
        def one(i):
            mask = jnp.where(lanes[...] == i, 1.0, 0.0).astype(BF16)
            dst[i] = (values[...] * mask[None]).reshape(TILE, tiles * TILE)

        loop(0, dst.shape[0], one)

    mask_tiles(by_row, a_cat, row_lanes)
    for h in range(halves):
        space[h][pl.ds(0, first_halo)] = features[:, h * TILE : (h + 1) * TILE].reshape(
            first_halo, CAP, TILE
        )
        space[h][first_halo + d] = jnp.zeros((CAP, TILE), BF16)
        back_recv[h, d] = jnp.zeros((CAP, TILE), BF16)
    mask_tiles(by_column, at_cat, column_lanes)

    def make_scatter(block):
        rows_of = listed[block].T
        for i in range(row_tiles):
            scatter[i, block] = jnp.where(rows_of == row + i * TILE, 1.0, 0.0).astype(BF16)

    loop(0, blocks, make_scatter)

    def tile_sum(values, h):
        return jnp.dot(values, picked[h], preferred_element_type=F32)

    own = []
    for h in range(halves):
        await_bytes(space[h].at[pl.ds(first_halo, doms - 1)], recv_sems, HALO + h)
        for t in range(tiles):
            picked[h, t * TILE : (t + 1) * TILE, :] = space[h][
                pl.ds(tile_column[0, 0, t] * per, per)
            ].reshape(TILE, TILE)
        for k in far_reps:
            i = lax.rem(r + k, reps)
            agg_send[h, i] = tile_sum(by_row[i], h).astype(BF16)
            push(agg_send.at[h, i], agg_recv.at[h, r], AGG + h, {"rep": i})
        own.append(tile_sum(by_row[r], h))

    def rep_sum(total, received, phase, h):
        await_bytes(received.at[h, pl.ds(0, reps - 1)], recv_sems, phase + h)
        for k in range(1, reps):
            total = total + received[h, lax.rem(r + k, reps)].astype(F32)
        return total

    aggregate = jnp.concatenate(
        [rep_sum(own[h], agg_recv, AGG, h).astype(BF16) for h in range(halves)], axis=1
    )

    pre_act = lax.dot_general(
        aggregate, weight[...], (((1,), (1,)), ((), ())), preferred_element_type=F32
    )
    activated, derivative = gelu_pair(pre_act)
    pre_grad = (cotangent[...].astype(F32) * derivative).astype(BF16)
    for h in range(halves):
        row_grads[h][r] = jnp.dot(
            pre_grad, weight[:, h * TILE : (h + 1) * TILE], preferred_element_type=F32
        ).astype(BF16)
        for k in far_reps:
            push(
                row_grads[h].at[r], row_grads[h].at[r], GRAD + h, {"rep": lax.rem(r + k, reps)}
            )
    output[...] = activated.astype(BF16)

    w_part = lax.dot_general(
        pre_grad, aggregate, (((0,), (0,)), ((), ())), preferred_element_type=F32
    )
    chunk = w_send.shape[1]
    half = doms // 2
    for h in range(2):
        w_send[h * half : (h + 1) * half] = w_part[:, h * TILE : (h + 1) * TILE].reshape(
            half, chunk, TILE
        )
    loop(0, blocks, lambda b: send_block(far_block(b), w_send, w_recv.at[d], W_DOM))
    w_recv[d] = w_send[d]

    for h in range(halves):
        await_bytes(row_grads[h].at[pl.ds(0, reps - 1)], recv_sems, GRAD + h)
        for t in range(tiles):
            picked[h, t * TILE : (t + 1) * TILE, :] = row_grads[h][tile_row[0, 0, t]]

        def backward_halo(b):
            block = far_block(b)
            grads = tile_sum(by_column[block + row_tiles], h).astype(BF16)
            back_send[h, pl.ds(block * per, per)] = grads.reshape(per, CAP, TILE)
            send_block(block, back_send.at[h], back_recv.at[h, d], BACK + h)

        loop(0, blocks, backward_halo)

    spread = half // reps
    holder = lax.rem(d, half) // spread
    place = (d // half) * spread + lax.rem(d, spread)
    await_bytes(w_recv.at[pl.ds(0, doms - 1)], recv_sems, W_DOM)
    w_sum[...] = jnp.sum(w_recv[...], axis=0)

    @pl.when(r != holder)
    def _():
        push(w_sum, w_rep.at[r], W_REP, {"rep": holder})

    for h in range(halves):

        def backward_local(i):
            feature_part[h, i] = tile_sum(by_column[i], h)

        loop(0, row_tiles, backward_local)

    @pl.when(r == holder)
    def _():
        await_bytes(w_rep.at[pl.ds(0, reps - 1)], recv_sems, W_REP)
        whole = w_sum[...]
        for k in range(1, reps):
            whole = whole + w_rep[lax.rem(r + k, reps)]
        w_done[place] = whole * scale

        def share_done(k):
            push(w_done.at[place], w_done.at[place], W_END, {"dom": lax.rem(d + k, doms)})

        loop(1, doms, share_done)

    own = []
    for h in range(halves):
        await_bytes(back_recv.at[h, pl.ds(0, doms - 1)], recv_sems, BACK + h)

        def feature_rows(i):
            total = feature_part[h, i]
            for block in range(blocks):
                returned = back_recv[h, block * per : (block + 1) * per].reshape(TILE, TILE)
                total = total + jnp.dot(scatter[i, block], returned, preferred_element_type=F32)
            return total

        for k in far_reps:
            i = lax.rem(r + k, reps)
            feat_send[h, i] = feature_rows(i).astype(BF16)
            push(feat_send.at[h, i], feat_recv.at[h, r], FEAT + h, {"rep": i})
        own.append(feature_rows(r))

    @pl.when(r == holder)
    def _():
        await_bytes(w_done.at[pl.ds(0, 2 * spread - 1)], recv_sems, W_END)

    @pl.when(r != holder)
    def _():
        await_bytes(w_done, recv_sems, W_END)

    for h in range(2):
        weight_grad[:, h * TILE : (h + 1) * TILE] = w_done[h * spread : (h + 1) * spread].reshape(
            spread * chunk, TILE
        )
    for h in range(halves):
        feature_grad[:, h * TILE : (h + 1) * TILE] = rep_sum(own[h], feat_recv, FEAT, h).astype(
            BF16
        )

    for h in range(halves):
        await_bytes(outgoing.at[h, pl.ds(0, doms - 1)], send_sems, HALO + h)
        await_bytes(agg_send.at[h, pl.ds(0, reps - 1)], send_sems, AGG + h)
        await_bytes(row_grads[h].at[pl.ds(0, reps - 1)], send_sems, GRAD + h)
        await_bytes(back_send.at[h, pl.ds(0, doms - 1)], send_sems, BACK + h)
        await_bytes(feat_send.at[h, pl.ds(0, reps - 1)], send_sems, FEAT + h)
    await_bytes(w_send.at[pl.ds(0, doms - 1)], send_sems, W_DOM)

    @pl.when(r != holder)
    def _():
        await_bytes(w_sum, send_sems, W_REP)

    @pl.when(r == holder)
    def _():
        await_bytes(w_send.at[pl.ds(0, doms - 1)], send_sems, W_END)


def solution(mesh):
    doms, reps = mesh.shape["dom"], mesh.shape["rep"]

    def local(
        features,
        weight,
        adjacency,
        tile_row,
        tile_column,
        tile_counts,
        send_rows,
        send_counts,
        cotangent,
    ):
        rows, hidden = features.shape
        tiles = adjacency.shape[2]
        row_tiles = rows // TILE
        blocks = doms * CAP // TILE
        halves = hidden // TILE
        chunk = 2 * hidden // doms
        vmem = pl.BlockSpec(memory_space=pltpu.VMEM)
        hbm = pl.BlockSpec(memory_space=pltpu.HBM)
        i32 = jnp.int32
        phases = halves * 5 + 3
        scratch = (
            ((rows, hidden), BF16),
            ((hidden, hidden), BF16),
            ((tiles, TILE, TILE), BF16),
            ((CAP, doms), i32),
            ((1, doms), i32),
            (pltpu.SMEM, (1, 1, tiles), i32),
            (pltpu.SMEM, (1, 1, tiles), i32),
            (pltpu.SMEM, (1, 1), i32),
            ((rows // reps, hidden), BF16),
            ((blocks, TILE, TILE), i32),
            ((rows // CAP + doms, CAP, TILE), BF16),
            ((rows // CAP + doms, CAP, TILE), BF16),
            ((halves, doms, CAP, TILE), BF16),
            ((row_tiles, blocks, TILE, TILE), BF16),
            ((TILE // CAP, CAP, tiles * TILE), BF16),
            ((TILE // CAP, CAP, tiles * TILE), BF16),
            ((row_tiles, TILE, tiles * TILE), BF16),
            ((row_tiles + blocks, TILE, tiles * TILE), BF16),
            ((CAP, tiles * TILE), i32),
            ((CAP, tiles * TILE), i32),
            ((halves, tiles * TILE, TILE), BF16),
            ((halves, reps, TILE, TILE), BF16),
            ((halves, reps, TILE, TILE), BF16),
            ((reps, TILE, TILE), BF16),
            ((reps, TILE, TILE), BF16),
            ((halves, doms, CAP, TILE), BF16),
            ((halves, doms, CAP, TILE), BF16),
            ((halves, row_tiles, TILE, TILE), F32),
            ((halves, reps, TILE, TILE), BF16),
            ((halves, reps, TILE, TILE), BF16),
            ((doms, chunk, TILE), F32),
            ((doms, chunk, TILE), F32),
            ((chunk, TILE), F32),
            ((reps, chunk, TILE), F32),
            ((doms // reps, chunk, TILE), F32),
        )
        return pl.pallas_call(
            functools.partial(kernel, doms, reps, float(rows * doms) ** (-0.5)),
            out_shape=(
                jax.ShapeDtypeStruct((rows // reps, hidden), BF16),
                jax.ShapeDtypeStruct((rows // reps, hidden), BF16),
                jax.ShapeDtypeStruct((hidden // reps, hidden), F32),
            ),
            in_specs=[hbm] * 9,
            out_specs=(vmem, vmem, vmem),
            scratch_shapes=[
                item[0](*item[1:]) if len(item) == 3 else pltpu.VMEM(*item) for item in scratch
            ]
            + [
                pltpu.SemaphoreType.DMA((9,)),
                pltpu.SemaphoreType.DMA((phases,)),
                pltpu.SemaphoreType.DMA((phases,)),
            ],
            compiler_params=pltpu.CompilerParams(
                collective_id=0, has_side_effects=True, vmem_limit_bytes=60 * 2**20
            ),
        )(
            features,
            weight,
            adjacency,
            jnp.swapaxes(send_rows, 2, 3),
            send_counts,
            tile_row,
            tile_column,
            tile_counts,
            cotangent,
        )

    in_specs = (
        P("dom", None),
        P(),
        P("dom", "rep", None, None, None),
        P("dom", "rep", None),
        P("dom", "rep", None),
        P("dom", "rep"),
        P("dom", "rep", None, None),
        P("dom", "rep", None),
        P(("dom", "rep"), None),
    )
    out_specs = (P(("dom", "rep"), None), P(("dom", "rep"), None), P("rep", None))
    return jax.shard_map(local, mesh=mesh, in_specs=in_specs, out_specs=out_specs, check_vma=False)
```

time: 103 us -> 81.1 us (0.79); the launches traced: 102 us -> 80.8 us
  Pallas kernels: 91.8 us -> 76.7 us
  local copies, waits for them, and re-layouts: 7.14 us -> 2.88 us
  other arithmetic: 1.32 us -> 0 us
    pallas_call x1, Pallas kernels: 91.8 us -> 76.7 us  [local(): pl.pallas_call(functools.partial(kernel, doms, reps, float(rows * doms) *...]
    unnamed x17 -> x7, local copies, waits for them, and re-layouts: 6.75 us -> 2.88 us
    unnamed x1 -> x0, other arithmetic: 1.32 us -> none
where the time goes in v2:
time: 81.1 us; the launch traced here: 80.8 us
  Pallas kernels  76.7 us (95%)
  local copies, waits for them, and re-layouts  2.88 us (4%)
  between operations  1.3 us (2%)
    pallas_call x1, Pallas kernels, local(): pl.pallas_call(functools.partial(kernel, doms, reps, float(rows * doms) *...  76.7 us
    unnamed x7, local copies, waits for them, and re-layouts  2.88 us

profile of v2, /device:TPU:1, one launch (start us, length us, event | category | flops | bytes accessed | tf_op | source)
XLA Modules:
  0.0 80.8 jit_solution(1077253635867950620)
XLA Ops:
  1.3 76.7 %shard_map.112 = (bf16[128,256]{1,0:T(8,128)(2,1)}, bf16[128,256]{1,0:T(8,128)(2,1)}, f32[32,256]{1,0:T(8,128)}) custom-call(bf16[1024,256]{1,0:T(8,128)(2,1)} %features_in.1, bf16[256,256]{1,0:T(8,128)(2,1)} %weight_in.1, bf16[1,1,16,128,128]{4,3,2,1,0:T(8,128)(2,1)} %adjacency_in.1, s32[1,1,16,64]{3,2,1,0:T(8,128)} %bitcast.1, s32[1,1,64]{2,1,0:T(1,128)} %list_counts_in.1, ...), custom_call_target="tpu_custom_call" | custom-call | tf_op jit(solution)/shard_map/pallas_call | solution.py:453
  78.0 0.0 copy-start
  78.0 1.5 %copy.16 = bf16[128,256]{1,0:T(8,128)(2,1)} copy(bf16[128,256]{1,0:T(8,128)(2,1)} %get-tuple-element.6) | data formatting | bytes 131072
  79.5 0.0 copy-done
  79.5 0.0 copy-start.1
  79.5 0.6 copy.17
  80.1 0.1 copy-done.1
  80.2 0.6 copy.18
Async XLA Ops:
  78.0 1.5 %copy-start = (bf16[128,256]{1,0:T(8,128)(2,1)S(1)}, bf16[128,256]{1,0:T(8,128)(2,1)}, u32[]{:S(2)}) copy-start(bf16[128,256]{1,0:T(8,128)(2,1)} %get-tuple-element.7) | copy-start | bytes 196612
  79.5 0.8 copy-start.1

commit v3 on v2

--- a/solution.py
+++ b/solution.py
@@ -73,6 +73,9 @@
     picked,
     agg_send,
     agg_recv,
+    own_sum,
+    aggregate,
+    pre_grad,
     row_grads_low,
     row_grads_high,
     back_send,
@@ -101,7 +104,7 @@
     space = (space_low, space_high)
     row_grads = (row_grads_low, row_grads_high)
     HALO, AGG, GRAD, BACK, FEAT = (halves * k for k in range(5))
-    W_DOM, W_REP, W_END = (halves * 5 + k for k in range(3))
+    W_DOM, W_REP, W_END, AGG_LAST = (halves * 5 + k for k in range(4))
 
     barrier = pltpu.get_barrier_semaphore()
 
@@ -114,9 +117,6 @@
         pl.semaphore_signal(
             barrier, inc=1, device_id={"rep": lax.rem(r + k, reps)}, device_id_type=MESH
         )
-
-    loop(1, doms, greet_dom)
-    loop(1, reps, greet_rep)
 
     loads = [
         pltpu.make_async_copy(src, dst, copy_sems.at[k])
@@ -134,7 +134,12 @@
             )
         )
     ]
-    for load in loads:
+    for load in loads[:3]:
+        load.start()
+    loop(doms // 2, doms, greet_dom)
+    loop(1, doms // 2, greet_dom)
+    loop(1, reps, greet_rep)
+    for load in loads[3:]:
         load.start()
 
     def push(src, dst, phase, target):
@@ -166,6 +171,11 @@
 
     far_reps = sorted(range(1, reps), key=lambda k: -min(k, reps - k))
 
+    def share_rows(h, k, c):
+        size = TILE // 2
+        mine = row_grads[h].at[r, c * size : (c + 1) * size]
+        push(mine, mine, GRAD + h, {"rep": lax.rem(r + k, reps)})
+
     lane = lax.broadcasted_iota(jnp.int32, (TILE, TILE), 1)
     row = lax.broadcasted_iota(jnp.int32, (TILE, TILE), 0)
     for load in loads[:3]:
@@ -192,17 +202,9 @@
     def send_halo(block, h):
         send_block(block, outgoing.at[h], space[h].at[first_halo + d], HALO + h)
 
-    gather(far_block(0))
+    loop(0, blocks, gather)
     pl.semaphore_wait(barrier, doms + reps - 2)
-    send_halo(far_block(0), 0)
-
-    def gather_and_send(b):
-        block = far_block(b)
-        gather(block)
-        send_halo(block, 0)
-
-    loop(1, blocks, gather_and_send)
-    for h in range(1, halves):
+    for h in range(halves):
         loop(0, blocks, lambda b: send_halo(far_block(b), h))
 
     for load in loads[3:]:
@@ -245,7 +247,19 @@
     def tile_sum(values, h):
         return jnp.dot(values, picked[h], preferred_element_type=F32)
 
-    own = []
+    pieces = 2
+    piece_rows = TILE // pieces
+    piece_at = [slice(c * piece_rows, (c + 1) * piece_rows) for c in range(pieces)]
+    last = halves - 1
+
+    def send_piece(h, i, c):
+        push(
+            agg_send.at[h, i, piece_at[c]],
+            agg_recv.at[h, r, piece_at[c]],
+            AGG_LAST + c if h == last else AGG + h,
+            {"rep": i},
+        )
+
     for h in range(halves):
         await_bytes(space[h].at[pl.ds(first_halo, doms - 1)], recv_sems, HALO + h)
         for t in range(tiles):
@@ -255,36 +269,49 @@
         for k in far_reps:
             i = lax.rem(r + k, reps)
             agg_send[h, i] = tile_sum(by_row[i], h).astype(BF16)
-            push(agg_send.at[h, i], agg_recv.at[h, r], AGG + h, {"rep": i})
-        own.append(tile_sum(by_row[r], h))
-
-    def rep_sum(total, received, phase, h):
-        await_bytes(received.at[h, pl.ds(0, reps - 1)], recv_sems, phase + h)
+            if h == last:
+                send_piece(h, i, 0)
+            else:
+                push(agg_send.at[h, i], agg_recv.at[h, r], AGG + h, {"rep": i})
+        if h == last:
+            for c in range(1, pieces):
+                for k in far_reps:
+                    send_piece(h, lax.rem(r + k, reps), c)
+        own_sum[h] = tile_sum(by_row[r], h)
+
+    for h in range(last):
+        await_bytes(agg_recv.at[h, pl.ds(0, reps - 1)], recv_sems, AGG + h)
         for k in range(1, reps):
-            total = total + received[h, lax.rem(r + k, reps)].astype(F32)
-        return total
-
-    aggregate = jnp.concatenate(
-        [rep_sum(own[h], agg_recv, AGG, h).astype(BF16) for h in range(halves)], axis=1
-    )
-
-    pre_act = lax.dot_general(
-        aggregate, weight[...], (((1,), (1,)), ((), ())), preferred_element_type=F32
-    )
-    activated, derivative = gelu_pair(pre_act)
-    pre_grad = (cotangent[...].astype(F32) * derivative).astype(BF16)
-    for h in range(halves):
-        row_grads[h][r] = jnp.dot(
-            pre_grad, weight[:, h * TILE : (h + 1) * TILE], preferred_element_type=F32
-        ).astype(BF16)
+            own_sum[h] += agg_recv[h, lax.rem(r + k, reps)].astype(F32)
+    for c in range(pieces):
+        await_bytes(agg_recv.at[last, pl.ds(0, reps - 1), piece_at[c]], recv_sems, AGG_LAST + c)
+        total = own_sum[last, piece_at[c]]
+        for k in range(1, reps):
+            total = total + agg_recv[last, lax.rem(r + k, reps), piece_at[c]].astype(F32)
+        piece = jnp.concatenate(
+            [own_sum[h, piece_at[c]].astype(BF16) for h in range(last)] + [total.astype(BF16)],
+            axis=1,
+        )
+        aggregate[piece_at[c]] = piece
+        pre_act = lax.dot_general(
+            piece, weight[...], (((1,), (1,)), ((), ())), preferred_element_type=F32
+        )
+        activated, derivative = gelu_pair(pre_act)
+        grad = (cotangent[piece_at[c]].astype(F32) * derivative).astype(BF16)
+        pre_grad[piece_at[c]] = grad
+        output[piece_at[c]] = activated.astype(BF16)
+        row_grad = jnp.dot(grad, weight[...], preferred_element_type=F32).astype(BF16)
+        for h in range(halves):
+            row_grads[h][r, piece_at[c]] = row_grad[:, h * TILE : (h + 1) * TILE]
         for k in far_reps:
-            push(
-                row_grads[h].at[r], row_grads[h].at[r], GRAD + h, {"rep": lax.rem(r + k, reps)}
-            )
-    output[...] = activated.astype(BF16)
+            share_rows(0, k, c)
+    for h in range(1, halves):
+        for c in range(pieces):
+            for k in far_reps:
+                share_rows(h, k, c)
 
     w_part = lax.dot_general(
-        pre_grad, aggregate, (((0,), (0,)), ((), ())), preferred_element_type=F32
+        pre_grad[...], aggregate[...], (((0,), (0,)), ((), ())), preferred_element_type=F32
     )
     chunk = w_send.shape[1]
     half = doms // 2
@@ -368,16 +395,21 @@
             spread * chunk, TILE
         )
     for h in range(halves):
-        feature_grad[:, h * TILE : (h + 1) * TILE] = rep_sum(own[h], feat_recv, FEAT, h).astype(
-            BF16
-        )
+        await_bytes(feat_recv.at[h, pl.ds(0, reps - 1)], recv_sems, FEAT + h)
+        total = own[h]
+        for k in range(1, reps):
+            total = total + feat_recv[h, lax.rem(r + k, reps)].astype(F32)
+        feature_grad[:, h * TILE : (h + 1) * TILE] = total.astype(BF16)
 
     for h in range(halves):
         await_bytes(outgoing.at[h, pl.ds(0, doms - 1)], send_sems, HALO + h)
-        await_bytes(agg_send.at[h, pl.ds(0, reps - 1)], send_sems, AGG + h)
+        if h != last:
+            await_bytes(agg_send.at[h, pl.ds(0, reps - 1)], send_sems, AGG + h)
         await_bytes(row_grads[h].at[pl.ds(0, reps - 1)], send_sems, GRAD + h)
         await_bytes(back_send.at[h, pl.ds(0, doms - 1)], send_sems, BACK + h)
         await_bytes(feat_send.at[h, pl.ds(0, reps - 1)], send_sems, FEAT + h)
+    for c in range(pieces):
+        await_bytes(agg_send.at[last, pl.ds(0, reps - 1), piece_at[c]], send_sems, AGG_LAST + c)
     await_bytes(w_send.at[pl.ds(0, doms - 1)], send_sems, W_DOM)
 
     @pl.when(r != holder)
@@ -412,7 +444,12 @@
         vmem = pl.BlockSpec(memory_space=pltpu.VMEM)
         hbm = pl.BlockSpec(memory_space=pltpu.HBM)
         i32 = jnp.int32
-        phases = halves * 5 + 3
+        phases = halves * 5 + 5
+        out_shape = (
+            jax.ShapeDtypeStruct((rows // reps, hidden), BF16),
+            jax.ShapeDtypeStruct((rows // reps, hidden), BF16),
+            jax.ShapeDtypeStruct((hidden // reps, hidden), F32),
+        )
         scratch = (
             ((rows, hidden), BF16),
             ((hidden, hidden), BF16),
@@ -437,6 +474,9 @@
             ((halves, tiles * TILE, TILE), BF16),
             ((halves, reps, TILE, TILE), BF16),
             ((halves, reps, TILE, TILE), BF16),
+            ((halves, TILE, TILE), F32),
+            ((TILE, hidden), BF16),
+            ((TILE, hidden), BF16),
             ((reps, TILE, TILE), BF16),
             ((reps, TILE, TILE), BF16),
             ((halves, doms, CAP, TILE), BF16),
@@ -452,13 +492,9 @@
         )
         return pl.pallas_call(
             functools.partial(kernel, doms, reps, float(rows * doms) ** (-0.5)),
-            out_shape=(
-                jax.ShapeDtypeStruct((rows // reps, hidden), BF16),
-                jax.ShapeDtypeStruct((rows // reps, hidden), BF16),
-                jax.ShapeDtypeStruct((hidden // reps, hidden), F32),
-            ),
+            out_shape=out_shape,
             in_specs=[hbm] * 9,
-            out_specs=(vmem, vmem, vmem),
+            out_specs=(vmem,) * 3,
             scratch_shapes=[
                 item[0](*item[1:]) if len(item) == 3 else pltpu.VMEM(*item) for item in scratch
             ]

time: 81.1 us -> 79.3 us (0.978)
  Pallas kernels: 76.7 us -> 74.5 us
    pallas_call x1, Pallas kernels: 76.7 us -> 74.5 us  [local(): pl.pallas_call(functools.partial(kernel, doms, reps, float(rows * doms) *...]
where the time goes in v3:
time: 79.3 us; the launch traced here: 78.6 us
  Pallas kernels  74.5 us (94%)
  local copies, waits for them, and re-layouts  2.88 us (4%)
  between operations  1.3 us (2%)
    pallas_call x1, Pallas kernels, local(): pl.pallas_call(functools.partial(kernel, doms, reps, float(rows * doms) *...  74.5 us
    unnamed x7, local copies, waits for them, and re-layouts  2.88 us

profile of v3, /device:TPU:1, one launch (start us, length us, event | category | flops | bytes accessed | tf_op | source)
XLA Modules:
  0.0 78.6 jit_solution(2181339469722777014)
XLA Ops:
  1.3 74.5 %shard_map.112 = (bf16[128,256]{1,0:T(8,128)(2,1)}, bf16[128,256]{1,0:T(8,128)(2,1)}, f32[32,256]{1,0:T(8,128)}) custom-call(bf16[1024,256]{1,0:T(8,128)(2,1)} %features_in.1, bf16[256,256]{1,0:T(8,128)(2,1)} %weight_in.1, bf16[1,1,16,128,128]{4,3,2,1,0:T(8,128)(2,1)} %adjacency_in.1, s32[1,1,16,64]{3,2,1,0:T(8,128)} %bitcast.1, s32[1,1,64]{2,1,0:T(1,128)} %list_counts_in.1, ...), custom_call_target="tpu_custom_call" | custom-call | tf_op jit(solution)/shard_map/pallas_call | solution.py:493
  75.7 0.0 copy-start
  75.7 1.5 %copy.16 = bf16[128,256]{1,0:T(8,128)(2,1)} copy(bf16[128,256]{1,0:T(8,128)(2,1)} %get-tuple-element.6) | data formatting | bytes 131072
  77.3 0.0 copy-done
  77.3 0.0 copy-start.1
  77.3 0.6 copy.17
  77.9 0.1 copy-done.1
  78.0 0.6 copy.18
Async XLA Ops:
  75.7 1.5 %copy-start = (bf16[128,256]{1,0:T(8,128)(2,1)S(1)}, bf16[128,256]{1,0:T(8,128)(2,1)}, u32[]{:S(2)}) copy-start(bf16[128,256]{1,0:T(8,128)(2,1)} %get-tuple-element.7) | copy-start | bytes 196612
  77.3 0.8 copy-start.1

commit v4 on v3

--- a/solution.py
+++ b/solution.py
@@ -335,6 +335,12 @@
 
         loop(0, blocks, backward_halo)
 
+        def backward_local(i):
+            pair = by_column[pl.ds(2 * i, 2)].reshape(2 * TILE, tiles * TILE)
+            feature_part[h, pl.ds(2 * i, 2)] = tile_sum(pair, h).reshape(2, TILE, TILE)
+
+        loop(0, row_tiles // 2, backward_local)
+
     spread = half // reps
     holder = lax.rem(d, half) // spread
     place = (d // half) * spread + lax.rem(d, spread)
@@ -345,25 +351,19 @@
     def _():
         push(w_sum, w_rep.at[r], W_REP, {"rep": holder})
 
-    for h in range(halves):
-
-        def backward_local(i):
-            feature_part[h, i] = tile_sum(by_column[i], h)
-
-        loop(0, row_tiles, backward_local)
-
-    @pl.when(r == holder)
-    def _():
-        await_bytes(w_rep.at[pl.ds(0, reps - 1)], recv_sems, W_REP)
-        whole = w_sum[...]
-        for k in range(1, reps):
-            whole = whole + w_rep[lax.rem(r + k, reps)]
-        w_done[place] = whole * scale
-
-        def share_done(k):
-            push(w_done.at[place], w_done.at[place], W_END, {"dom": lax.rem(d + k, doms)})
-
-        loop(1, doms, share_done)
+    def finish_weight():
+        @pl.when(r == holder)
+        def _():
+            await_bytes(w_rep.at[pl.ds(0, reps - 1)], recv_sems, W_REP)
+            whole = w_sum[...]
+            for k in range(1, reps):
+                whole = whole + w_rep[lax.rem(r + k, reps)]
+            w_done[place] = whole * scale
+
+            def share_done(k):
+                push(w_done.at[place], w_done.at[place], W_END, {"dom": lax.rem(d + k, doms)})
+
+            loop(1, doms, share_done)
 
     own = []
     for h in range(halves):
@@ -381,6 +381,8 @@
             feat_send[h, i] = feature_rows(i).astype(BF16)
             push(feat_send.at[h, i], feat_recv.at[h, r], FEAT + h, {"rep": i})
         own.append(feature_rows(r))
+        if h == 0:
+            finish_weight()
 
     @pl.when(r == holder)
     def _():

time: 79.3 us -> 76.5 us (0.965)
  Pallas kernels: 74.5 us -> 72.1 us
    pallas_call x1, Pallas kernels: 74.5 us -> 72.1 us  [local(): pl.pallas_call(functools.partial(kernel, doms, reps, float(rows * doms) *...]
where the time goes in v4:
time: 76.5 us; the launch traced here: 76.3 us
  Pallas kernels  72.1 us (94%)
  local copies, waits for them, and re-layouts  2.88 us (4%)
  between operations  1.3 us (2%)
    pallas_call x1, Pallas kernels, local(): pl.pallas_call(functools.partial(kernel, doms, reps, float(rows * doms) *...  72.1 us
    unnamed x7, local copies, waits for them, and re-layouts  2.88 us

profile of v4, /device:TPU:1, one launch (start us, length us, event | category | flops | bytes accessed | tf_op | source)
XLA Modules:
  0.0 76.3 jit_solution(17954270586696017638)
XLA Ops:
  1.3 72.1 %shard_map.112 = (bf16[128,256]{1,0:T(8,128)(2,1)}, bf16[128,256]{1,0:T(8,128)(2,1)}, f32[32,256]{1,0:T(8,128)}) custom-call(bf16[1024,256]{1,0:T(8,128)(2,1)} %features_in.1, bf16[256,256]{1,0:T(8,128)(2,1)} %weight_in.1, bf16[1,1,16,128,128]{4,3,2,1,0:T(8,128)(2,1)} %adjacency_in.1, s32[1,1,16,64]{3,2,1,0:T(8,128)} %bitcast.1, s32[1,1,64]{2,1,0:T(1,128)} %list_counts_in.1, ...), custom_call_target="tpu_custom_call" | custom-call | tf_op jit(solution)/shard_map/pallas_call | solution.py:495
  73.4 0.0 copy-start
  73.4 1.5 %copy.16 = bf16[128,256]{1,0:T(8,128)(2,1)} copy(bf16[128,256]{1,0:T(8,128)(2,1)} %get-tuple-element.6) | data formatting | bytes 131072
  74.9 0.0 copy-done
  74.9 0.0 copy-start.1
  74.9 0.6 copy.17
  75.5 0.1 copy-done.1
  75.6 0.6 copy.18
Async XLA Ops:
  73.4 1.5 %copy-start = (bf16[128,256]{1,0:T(8,128)(2,1)S(1)}, bf16[128,256]{1,0:T(8,128)(2,1)}, u32[]{:S(2)}) copy-start(bf16[128,256]{1,0:T(8,128)(2,1)} %get-tuple-element.7) | copy-start | bytes 196612
  74.9 0.8 copy-start.1

commit v5 on v4

--- a/solution.py
+++ b/solution.py
@@ -47,6 +47,9 @@
     tile_column_in,
     tile_count_in,
     cotangent_in,
+    output_out,
+    feature_grad_out,
+    weight_grad_out,
     output,
     feature_grad,
     weight_grad,
@@ -310,6 +313,14 @@
             for k in far_reps:
                 share_rows(h, k, c)
 
+    stores = [
+        pltpu.make_async_copy(src, dst, copy_sems.at[len(loads) + k])
+        for k, (src, dst) in enumerate(
+            ((output, output_out), (weight_grad, weight_grad_out), (feature_grad, feature_grad_out))
+        )
+    ]
+    stores[0].start()
+
     w_part = lax.dot_general(
         pre_grad[...], aggregate[...], (((0,), (0,)), ((), ())), preferred_element_type=F32
     )
@@ -396,12 +407,15 @@
         weight_grad[:, h * TILE : (h + 1) * TILE] = w_done[h * spread : (h + 1) * spread].reshape(
             spread * chunk, TILE
         )
+    stores[1].start()
     for h in range(halves):
         await_bytes(feat_recv.at[h, pl.ds(0, reps - 1)], recv_sems, FEAT + h)
         total = own[h]
         for k in range(1, reps):
             total = total + feat_recv[h, lax.rem(r + k, reps)].astype(F32)
         feature_grad[:, h * TILE : (h + 1) * TILE] = total.astype(BF16)
+
+    stores[2].start()
 
     for h in range(halves):
         await_bytes(outgoing.at[h, pl.ds(0, doms - 1)], send_sems, HALO + h)
@@ -421,6 +435,22 @@
     @pl.when(r == holder)
     def _():
         await_bytes(w_send.at[pl.ds(0, doms - 1)], send_sems, W_END)
+
+    for store in stores:
+        store.wait()
+
+
+def hand_over(*refs):
+    made, results, held, sems = refs[:3], refs[3:6], refs[6:9], refs[9]
+    loads = [pltpu.make_async_copy(made[k], held[k], sems.at[k]) for k in range(3)]
+    stores = [pltpu.make_async_copy(held[k], results[k], sems.at[3 + k]) for k in range(3)]
+    for load in loads:
+        load.start()
+    for load, store in zip(loads, stores):
+        load.wait()
+        store.start()
+    for store in stores:
+        store.wait()
 
 
 def solution(mesh):
@@ -443,7 +473,6 @@
         blocks = doms * CAP // TILE
         halves = hidden // TILE
         chunk = 2 * hidden // doms
-        vmem = pl.BlockSpec(memory_space=pltpu.VMEM)
         hbm = pl.BlockSpec(memory_space=pltpu.HBM)
         i32 = jnp.int32
         phases = halves * 5 + 5
@@ -452,6 +481,7 @@
             jax.ShapeDtypeStruct((rows // reps, hidden), BF16),
             jax.ShapeDtypeStruct((hidden // reps, hidden), F32),
         )
+        staged = [pltpu.VMEM(leaf.shape, leaf.dtype) for leaf in out_shape]
         scratch = (
             ((rows, hidden), BF16),
             ((hidden, hidden), BF16),
@@ -492,16 +522,17 @@
             ((reps, chunk, TILE), F32),
             ((doms // reps, chunk, TILE), F32),
         )
-        return pl.pallas_call(
+        made = pl.pallas_call(
             functools.partial(kernel, doms, reps, float(rows * doms) ** (-0.5)),
             out_shape=out_shape,
             in_specs=[hbm] * 9,
-            out_specs=(vmem,) * 3,
-            scratch_shapes=[
+            out_specs=(hbm,) * 3,
+            scratch_shapes=staged
+            + [
                 item[0](*item[1:]) if len(item) == 3 else pltpu.VMEM(*item) for item in scratch
             ]
             + [
-                pltpu.SemaphoreType.DMA((9,)),
+                pltpu.SemaphoreType.DMA((12,)),
                 pltpu.SemaphoreType.DMA((phases,)),
                 pltpu.SemaphoreType.DMA((phases,)),
             ],
@@ -519,6 +550,14 @@
             tile_counts,
             cotangent,
         )
+        return pl.pallas_call(
+            hand_over,
+            out_shape=out_shape,
+            in_specs=[hbm] * 3,
+            out_specs=(hbm,) * 3,
+            scratch_shapes=staged + [pltpu.SemaphoreType.DMA((6,))],
+            compiler_params=pltpu.CompilerParams(vmem_limit_bytes=60 * 2**20),
+        )(*made)
 
     in_specs = (
         P("dom", None),

time: 76.5 us -> 75.1 us (0.982)
  local copies, waits for them, and re-layouts: 2.88 us -> 0 us
  Pallas kernels: 72.1 us -> 73.6 us
    unnamed x7 -> x0, local copies, waits for them, and re-layouts: 2.88 us -> none
    pallas_call x0 -> x1, Pallas kernels: none -> 1.56 us  [local(): pl.pallas_call(hand_over, out_shape=out_shape, in_specs=[hbm] * 3, out_sp...]
where the time goes in v5:
time: 75.1 us; the launch traced here: 74.9 us
  Pallas kernels  73.6 us (98%)
  between operations  1.29 us (2%)
    pallas_call x1, Pallas kernels, local(): pl.pallas_call(functools.partial(kernel, doms, reps, float(rows * doms) *...  72 us
    pallas_call x1, Pallas kernels, local(): pl.pallas_call(hand_over, out_shape=out_shape, in_specs=[hbm] * 3, out_sp...  1.56 us

profile of v5, /device:TPU:1, one launch (start us, length us, event | category | flops | bytes accessed | tf_op | source)
XLA Modules:
  0.0 74.9 jit_solution(2108338177489557673)
XLA Ops:
  1.3 72.0 %shard_map.112 = (bf16[128,256]{1,0:T(8,128)(2,1)}, bf16[128,256]{1,0:T(8,128)(2,1)}, f32[32,256]{1,0:T(8,128)}) custom-call(bf16[1024,256]{1,0:T(8,128)(2,1)} %features_in.1, bf16[256,256]{1,0:T(8,128)(2,1)} %weight_in.1, bf16[1,1,16,128,128]{4,3,2,1,0:T(8,128)(2,1)} %adjacency_in.1, s32[1,1,16,64]{3,2,1,0:T(8,128)} %bitcast.1, s32[1,1,64]{2,1,0:T(1,128)} %list_counts_in.1, ...), custom_call_target="tpu_custom_call" | custom-call | tf_op jit(solution)/shard_map/pallas_call | solution.py:525
  73.3 1.6 %shard_map.113 = (bf16[128,256]{1,0:T(8,128)(2,1)}, bf16[128,256]{1,0:T(8,128)(2,1)}, f32[32,256]{1,0:T(8,128)}) custom-call(bf16[128,256]{1,0:T(8,128)(2,1)} %get-tuple-element.6.refs_0_, bf16[128,256]{1,0:T(8,128)(2,1)} %get-tuple-element.7.refs_1_, f32[32,256]{1,0:T(8,128)} %get-tuple-element.8.refs_2_), custom_call_target="tpu_custom_call" | custom-call | tf_op jit(solution)/shard_map/pallas_call | solution.py:553

commit v6 on v5

--- a/solution.py
+++ b/solution.py
@@ -333,24 +333,32 @@
     loop(0, blocks, lambda b: send_block(far_block(b), w_send, w_recv.at[d], W_DOM))
     w_recv[d] = w_send[d]
 
+    def backward_local(h):
+        def some(i):
+            pair = by_column[pl.ds(2 * i, 2)].reshape(2 * TILE, tiles * TILE)
+            feature_part[h, pl.ds(2 * i, 2)] = tile_sum(pair, h).reshape(2, TILE, TILE)
+
+        loop(0, row_tiles // 2, some)
+
+    group = 2 - blocks % 2
     for h in range(halves):
         await_bytes(row_grads[h].at[pl.ds(0, reps - 1)], recv_sems, GRAD + h)
         for t in range(tiles):
             picked[h, t * TILE : (t + 1) * TILE, :] = row_grads[h][tile_row[0, 0, t]]
 
         def backward_halo(b):
-            block = far_block(b)
-            grads = tile_sum(by_column[block + row_tiles], h).astype(BF16)
-            back_send[h, pl.ds(block * per, per)] = grads.reshape(per, CAP, TILE)
-            send_block(block, back_send.at[h], back_recv.at[h, d], BACK + h)
-
-        loop(0, blocks, backward_halo)
-
-        def backward_local(i):
-            pair = by_column[pl.ds(2 * i, 2)].reshape(2 * TILE, tiles * TILE)
-            feature_part[h, pl.ds(2 * i, 2)] = tile_sum(pair, h).reshape(2, TILE, TILE)
-
-        loop(0, row_tiles // 2, backward_local)
+            some = [far_block(group * b + k) for k in range(group)]
+            columns = jnp.concatenate([by_column[block + row_tiles] for block in some], axis=0)
+            grads = tile_sum(columns, h).astype(BF16)
+            for k, block in enumerate(some):
+                back_send[h, pl.ds(block * per, per)] = grads[k * TILE : (k + 1) * TILE].reshape(
+                    per, CAP, TILE
+                )
+                send_block(block, back_send.at[h], back_recv.at[h, d], BACK + h)
+
+        loop(0, blocks // group, backward_halo)
+        if h == 0:
+            backward_local(h)
 
     spread = half // reps
     holder = lax.rem(d, half) // spread
@@ -394,6 +402,8 @@
         own.append(feature_rows(r))
         if h == 0:
             finish_weight()
+        if h < last:
+            backward_local(h + 1)
 
     @pl.when(r == holder)
     def _():

time: 75.1 us -> 74.3 us (0.989)
  Pallas kernels: 73.6 us -> 72.8 us
where the time goes in v6:
time: 74.3 us; the launch traced here: 74.1 us
  Pallas kernels  72.8 us (98%)
  between operations  1.29 us (2%)
    pallas_call x1, Pallas kernels, local(): pl.pallas_call(functools.partial(kernel, doms, reps, float(rows * doms) *...  71.3 us
    pallas_call x1, Pallas kernels, local(): pl.pallas_call(hand_over, out_shape=out_shape, in_specs=[hbm] * 3, out_sp...  1.56 us

profile of v6, /device:TPU:1, one launch (start us, length us, event | category | flops | bytes accessed | tf_op | source)
XLA Modules:
  0.0 74.1 jit_solution(6873108573745493913)
XLA Ops:
  1.3 71.3 %shard_map.112 = (bf16[128,256]{1,0:T(8,128)(2,1)}, bf16[128,256]{1,0:T(8,128)(2,1)}, f32[32,256]{1,0:T(8,128)}) custom-call(bf16[1024,256]{1,0:T(8,128)(2,1)} %features_in.1, bf16[256,256]{1,0:T(8,128)(2,1)} %weight_in.1, bf16[1,1,16,128,128]{4,3,2,1,0:T(8,128)(2,1)} %adjacency_in.1, s32[1,1,16,64]{3,2,1,0:T(8,128)} %bitcast.1, s32[1,1,64]{2,1,0:T(1,128)} %list_counts_in.1, ...), custom_call_target="tpu_custom_call" | custom-call | tf_op jit(solution)/shard_map/pallas_call | solution.py:535
  72.6 1.6 %shard_map.113 = (bf16[128,256]{1,0:T(8,128)(2,1)}, bf16[128,256]{1,0:T(8,128)(2,1)}, f32[32,256]{1,0:T(8,128)}) custom-call(bf16[128,256]{1,0:T(8,128)(2,1)} %get-tuple-element.6.refs_0_, bf16[128,256]{1,0:T(8,128)(2,1)} %get-tuple-element.7.refs_1_, f32[32,256]{1,0:T(8,128)} %get-tuple-element.8.refs_2_), custom_call_target="tpu_custom_call" | custom-call | tf_op jit(solution)/shard_map/pallas_call | solution.py:563

commit v7 on v6

--- a/solution.py
+++ b/solution.py
@@ -243,7 +243,9 @@
     def make_scatter(block):
         rows_of = listed[block].T
         for i in range(row_tiles):
-            scatter[i, block] = jnp.where(rows_of == row + i * TILE, 1.0, 0.0).astype(BF16)
+            scatter[i, :, pl.ds(pl.multiple_of(block * TILE, TILE), TILE)] = jnp.where(
+                rows_of == row + i * TILE, 1.0, 0.0
+            ).astype(BF16)
 
     loop(0, blocks, make_scatter)
 
@@ -389,11 +391,10 @@
         await_bytes(back_recv.at[h, pl.ds(0, doms - 1)], recv_sems, BACK + h)
 
         def feature_rows(i):
-            total = feature_part[h, i]
-            for block in range(blocks):
-                returned = back_recv[h, block * per : (block + 1) * per].reshape(TILE, TILE)
-                total = total + jnp.dot(scatter[i, block], returned, preferred_element_type=F32)
-            return total
+            returned = back_recv[h].reshape(doms * CAP, TILE)
+            return feature_part[h, i] + jnp.dot(
+                scatter[i], returned, preferred_element_type=F32
+            )
 
         for k in far_reps:
             i = lax.rem(r + k, reps)
@@ -506,7 +507,7 @@
             ((rows // CAP + doms, CAP, TILE), BF16),
             ((rows // CAP + doms, CAP, TILE), BF16),
             ((halves, doms, CAP, TILE), BF16),
-            ((row_tiles, blocks, TILE, TILE), BF16),
+            ((row_tiles, TILE, doms * CAP), BF16),
             ((TILE // CAP, CAP, tiles * TILE), BF16),
             ((TILE // CAP, CAP, tiles * TILE), BF16),
             ((row_tiles, TILE, tiles * TILE), BF16),

time: 74.3 us -> 74.2 us (level)
  no operation moved by 1% of the time
where the time goes in v7:
time: 74.2 us; the launch traced here: 74 us
  Pallas kernels  72.7 us (98%)
  between operations  1.29 us (2%)
    pallas_call x1, Pallas kernels, local(): pl.pallas_call(functools.partial(kernel, doms, reps, float(rows * doms) *...  71.1 us
    pallas_call x1, Pallas kernels, local(): pl.pallas_call(hand_over, out_shape=out_shape, in_specs=[hbm] * 3, out_sp...  1.56 us

profile of v7, /device:TPU:1, one launch (start us, length us, event | category | flops | bytes accessed | tf_op | source)
XLA Modules:
  0.0 74.0 jit_solution(13104198728316861655)
XLA Ops:
  1.3 71.1 %shard_map.112 = (bf16[128,256]{1,0:T(8,128)(2,1)}, bf16[128,256]{1,0:T(8,128)(2,1)}, f32[32,256]{1,0:T(8,128)}) custom-call(bf16[1024,256]{1,0:T(8,128)(2,1)} %features_in.1, bf16[256,256]{1,0:T(8,128)(2,1)} %weight_in.1, bf16[1,1,16,128,128]{4,3,2,1,0:T(8,128)(2,1)} %adjacency_in.1, s32[1,1,16,64]{3,2,1,0:T(8,128)} %bitcast.1, s32[1,1,64]{2,1,0:T(1,128)} %list_counts_in.1, ...), custom_call_target="tpu_custom_call" | custom-call | tf_op jit(solution)/shard_map/pallas_call | solution.py:536
  72.4 1.6 %shard_map.113 = (bf16[128,256]{1,0:T(8,128)(2,1)}, bf16[128,256]{1,0:T(8,128)(2,1)}, f32[32,256]{1,0:T(8,128)}) custom-call(bf16[128,256]{1,0:T(8,128)(2,1)} %get-tuple-element.6.refs_0_, bf16[128,256]{1,0:T(8,128)(2,1)} %get-tuple-element.7.refs_1_, f32[32,256]{1,0:T(8,128)} %get-tuple-element.8.refs_2_), custom_call_target="tpu_custom_call" | custom-call | tf_op jit(solution)/shard_map/pallas_call | solution.py:564

commit v8 on v7

--- a/solution.py
+++ b/solution.py
@@ -311,9 +311,9 @@
         for k in far_reps:
             share_rows(0, k, c)
     for h in range(1, halves):
-        for c in range(pieces):
-            for k in far_reps:
-                share_rows(h, k, c)
+        for k in far_reps:
+            mine = row_grads[h].at[r]
+            push(mine, mine, GRAD + h, {"rep": lax.rem(r + k, reps)})
 
     stores = [
         pltpu.make_async_copy(src, dst, copy_sems.at[len(loads) + k])

time: 74.2 us -> 75.3 us (1.015)
  Pallas kernels: 72.7 us -> 73.8 us
    pallas_call x1, Pallas kernels: 71.1 us -> 72.3 us  [local(): pl.pallas_call(functools.partial(kernel, doms, reps, float(rows * doms) *...]
where the time goes in v8:
time: 75.3 us; the launch traced here: 75.1 us
  Pallas kernels  73.8 us (98%)
  between operations  1.29 us (2%)
    pallas_call x1, Pallas kernels, local(): pl.pallas_call(functools.partial(kernel, doms, reps, float(rows * doms) *...  72.3 us
    pallas_call x1, Pallas kernels, local(): pl.pallas_call(hand_over, out_shape=out_shape, in_specs=[hbm] * 3, out_sp...  1.56 us

profile of v8, /device:TPU:1, one launch (start us, length us, event | category | flops | bytes accessed | tf_op | source)
XLA Modules:
  0.0 75.1 jit_solution(17788392451918699147)
XLA Ops:
  1.3 72.3 %shard_map.112 = (bf16[128,256]{1,0:T(8,128)(2,1)}, bf16[128,256]{1,0:T(8,128)(2,1)}, f32[32,256]{1,0:T(8,128)}) custom-call(bf16[1024,256]{1,0:T(8,128)(2,1)} %features_in.1, bf16[256,256]{1,0:T(8,128)(2,1)} %weight_in.1, bf16[1,1,16,128,128]{4,3,2,1,0:T(8,128)(2,1)} %adjacency_in.1, s32[1,1,16,64]{3,2,1,0:T(8,128)} %bitcast.1, s32[1,1,64]{2,1,0:T(1,128)} %list_counts_in.1, ...), custom_call_target="tpu_custom_call" | custom-call | tf_op jit(solution)/shard_map/pallas_call | solution.py:536
  73.6 1.6 %shard_map.113 = (bf16[128,256]{1,0:T(8,128)(2,1)}, bf16[128,256]{1,0:T(8,128)(2,1)}, f32[32,256]{1,0:T(8,128)}) custom-call(bf16[128,256]{1,0:T(8,128)(2,1)} %get-tuple-element.6.refs_0_, bf16[128,256]{1,0:T(8,128)(2,1)} %get-tuple-element.7.refs_1_, f32[32,256]{1,0:T(8,128)} %get-tuple-element.8.refs_2_), custom_call_target="tpu_custom_call" | custom-call | tf_op jit(solution)/shard_map/pallas_call | solution.py:564
